TPU v7x, 32 devices: a whole 2x2x4 slice. The times are simulated.
32 devices in a mesh: date: 8 (over z, y), strip: 4 (over x, core).
Axes of the slice: x: 2, y: 2, z: 4, core: 2. Of those that a mesh axis runs over, the one named last changes fastest.
Arguments:
- scenes: bfloat16 [2, 16, 128, 4096], P(None, 'date', 'strip'), may hold values from -6 to 6
- date_pairs: int32 [12, 2], replicated, may hold values from 0 to 15, as said below
- first_weight: bfloat16 [3, 3, 64, 2], replicated, may hold values from -4 to 4
- mid_weight: bfloat16 [2, 3, 3, 64, 64], replicated, may hold values from -0.375 to 0.375
- last_weight: bfloat16 [3, 3, 1, 64], replicated, may hold values from -0.375 to 0.375
- inversion: float32 [16, 12], replicated, may hold values from -1.75 to 1.75
Outputs:
- displacement: float32 [16, 32, 256], P('date', 'strip')
Inputs may be any that keep to these rules, and one draw needn't show every extreme that they name: `date_pairs`: Write g(d) = d // 2 for the date group of date d; in matching m, g of the reference date and g of the secondary date differ exactly in the bit of value step, and every group in 0..2 4 - 1 appears in exactly one interferogram of each matching. Which side is the reference and which date of a group is used vary.
All inputs are finite; a program needn't handle non-finite values.
Results may differ from a plain program's by a relative error of at most 0.02.
Values may be sent and summed in bfloat16 or wider, within the bound.
A program may use at most 64 MiB of HBM per device.

v0:
```python
import jax
import jax.numpy as jnp
from jax import lax
from jax.sharding import PartitionSpec as P

LOOK_R = 4
LOOK_C = 16


def from_partner(block, axis, apart):
    count = lax.axis_size(axis)
    route = []
    for low in range(count):
        high = low | 1 << apart
        if high != low and high < count:
            route += [(low, high), (high, low)]
    return lax.ppermute(block, axis, route)


def extended_2(block, sides, width):
    for axis, dim in sides:
        count = lax.axis_size(axis)
        forward = [(i, i + 1) for i in range(count - 1)]
        backward = [(target, source) for source, target in forward]
        low = lax.ppermute(
            lax.slice_in_dim(block, block.shape[dim] - width, None, axis=dim), axis, forward
        )
        high = lax.ppermute(lax.slice_in_dim(block, 0, width, axis=dim), axis, backward)
        block = jnp.concatenate([low, block, high], axis=dim)
    return block


def look_sum(field):
    lead = field.shape[:-2]
    count_rows = field.shape[-2]
    count_cols = field.shape[-1]
    shaped = field.reshape(lead + (count_rows // LOOK_R, LOOK_R, count_cols // LOOK_C, LOOK_C))
    return shaped.sum(axis=(-3, -1))


def coherence_of(first, second):
    first = first.astype(jnp.float32)
    second = second.astype(jnp.float32)
    real_part = first[0] * second[0] + first[1] * second[1]
    imag_part = first[1] * second[0] - first[0] * second[1]
    first_power = first[0] * first[0] + first[1] * first[1]
    second_power = second[0] * second[0] + second[1] * second[1]
    scale = lax.rsqrt(look_sum(first_power) * look_sum(second_power) + 1e-06)
    return (jnp.stack([look_sum(real_part), look_sum(imag_part)]) * scale).astype(jnp.bfloat16)


def convolve(padded, weight):
    count_rows = padded.shape[2] - 2
    count_cols = padded.shape[3] - 2
    total = None
    for tap_row in range(3):
        for tap_col in range(3):
            piece = padded[:, :, tap_row : tap_row + count_rows, tap_col : tap_col + count_cols]
            term = jnp.einsum(
                "oi,pirc->porc", weight[tap_row, tap_col], piece, preferred_element_type=jnp.float32
            )
            total = term if total is None else total + term
    return total


def side_columns(extended, is_lower, bit_pos):
    send = jnp.where(is_lower, extended[..., -1:], extended[..., :1])
    received = from_partner(send, "date", bit_pos)
    nothing = jnp.zeros_like(received)
    left_side = jnp.where(is_lower, nothing, received)
    right_side = jnp.where(is_lower, received, nothing)
    return jnp.concatenate([left_side, extended, right_side], axis=-1)


def per_device(scenes, date_pairs, first_weight, mid_weight, last_weight, inversion):
    date_dev = scenes.shape[1]
    count_cols = scenes.shape[3]
    half_cols = count_cols // 2
    dev_count = lax.axis_size("date")
    my_index = lax.axis_index("date")
    block_size = dev_count // 2
    bit_list = [0, 1, dev_count.bit_length() - 2]
    slot_iota = jnp.arange(block_size, dtype=jnp.int32)
    lower_flags = []
    pair_index = []
    inputs = []
    for which in range(3):
        bit_pos = bit_list[which]
        block_rows = date_pairs[which * block_size : (which + 1) * block_size]
        ref_group = block_rows[:, 0] // date_dev
        sec_group = block_rows[:, 1] // date_dev
        ref_hit = ref_group == my_index
        sec_hit = sec_group == my_index
        is_ref = jnp.any(ref_hit)
        my_date = jnp.sum(
            jnp.where(ref_hit, block_rows[:, 0], 0) + jnp.where(sec_hit, block_rows[:, 1], 0)
        )
        local_date = my_date - my_index * date_dev
        pair_index.append(which * block_size + jnp.sum(jnp.where(ref_hit | sec_hit, slot_iota, 0)))
        is_lower = my_index >> bit_pos & 1 == 0
        lower_flags.append(is_lower)
        date_tile = lax.dynamic_index_in_dim(scenes, local_date, 1, keepdims=False)
        own_half = jnp.where(is_lower, date_tile[..., :half_cols], date_tile[..., half_cols:])
        send_half = jnp.where(is_lower, date_tile[..., half_cols:], date_tile[..., :half_cols])
        other_half = from_partner(send_half, "date", bit_pos)
        first = jnp.where(is_ref, own_half, other_half)
        second = jnp.where(is_ref, other_half, own_half)
        inputs.append(coherence_of(first, second))
    stacked = jnp.stack(inputs)
    weights = (
        [first_weight] + [mid_weight[inner] for inner in range(mid_weight.shape[0])] + [last_weight]
    )
    layer_count = len(weights)
    hidden = stacked
    for depth_step in range(layer_count):
        extended = extended_2(hidden, (("strip", 2),), 1)
        padded = jnp.stack(
            [
                side_columns(extended[which], lower_flags[which], bit_list[which])
                for which in range(3)
            ]
        )
        result = convolve(padded, weights[depth_step])
        if depth_step + 1 < layer_count:
            hidden = jax.nn.relu(result).astype(jnp.bfloat16)
        else:
            hidden = result.astype(jnp.bfloat16)
    phases = hidden[:, 0]
    my_inversion = lax.dynamic_slice_in_dim(inversion, my_index * date_dev, date_dev, 0)
    group_iota = jnp.arange(dev_count, dtype=jnp.int32)
    table_parts = []
    side_parts = []
    for which in range(3):
        block_rows = date_pairs[which * block_size : (which + 1) * block_size]
        ref_group = block_rows[:, 0] // date_dev
        sec_group = block_rows[:, 1] // date_dev
        matched = (
            (ref_group[None, :] == group_iota[:, None])
            | (sec_group[None, :] == group_iota[:, None])
        ).astype(jnp.float32)
        block_inv = my_inversion[:, which * block_size : (which + 1) * block_size]
        table_parts.append(jnp.dot(matched, block_inv.T, precision=lax.Precision.HIGHEST))
        side_parts.append((group_iota >> bit_list[which] & 1 == 0).astype(jnp.float32))
    weight_table = jnp.stack(table_parts, axis=1).reshape(dev_count * 3, date_dev)
    side_table = jnp.stack(side_parts, axis=1).reshape(dev_count * 3)
    piece_float = lax.all_gather(phases, "date", axis=0, tiled=True).astype(jnp.float32)
    left_acc = jnp.einsum(
        "nd,nrc->drc",
        weight_table * side_table[:, None],
        piece_float,
        precision=lax.Precision.HIGHEST,
    )
    right_acc = jnp.einsum(
        "nd,nrc->drc",
        weight_table * (1.0 - side_table[:, None]),
        piece_float,
        precision=lax.Precision.HIGHEST,
    )
    left_acc, right_acc = (left_acc, right_acc)
    return jnp.concatenate([left_acc, right_acc], axis=-1)


def solution(mesh):
    return jax.shard_map(
        per_device,
        mesh=mesh,
        in_specs=(P(None, "date", "strip", None), P(), P(), P(), P(), P()),
        out_specs=P("date", "strip", None),
        check_vma=False,
    )
```

profile of v0, /device:TPU:2, one launch (start us, length us, event | category | flops | bytes accessed | tf_op | source)
XLA Modules:
  0.0 154.3 jit_solution(17376339891031271360)
XLA Ops:
  6.8 2.7 %collective-permute-start.2 = (bf16[2,32,2048]{2,1,0:T(8,128)(2,1)S(1)}, bf16[2,32,2048]{2,1,0:T(8,128)(2,1)S(1)}, u32[]{:S(2)}, u32[]{:S(2)}) collective-permute-start(bf16[2,32,2048]{2,1,0:T(8,128)(2,1)S(1)} %broadcast_select_fusion), channel_id=1, source_target_pairs={{0,16},{16,0},{4,20},{20,4},{8,24},{24,8},{12,28},{28,12},{1,17},{... | collective-permute-start | bytes 786440 | tf_op jit(solution)/shard_map/ppermute | solution.py:17
  12.5 1.9 %collective-permute-start.1 = (bf16[2,32,2048]{2,1,0:T(8,128)(2,1)}, bf16[2,32,2048]{2,1,0:T(8,128)(2,1)}, u32[]{:S(2)}, u32[]{:S(2)}) collective-permute-start(bf16[2,32,2048]{2,1,0:T(8,128)(2,1)} %broadcast_select_fusion.2), channel_id=1, source_target_pairs={{0,8},{8,0},{4,12},{12,4},{16,24},{24,16},{20,28},{28,20},{1,9},{9... | collective-permute-start | bytes 786440 | tf_op jit(solution)/shard_map/ppermute | solution.py:17
  15.3 6.3 %collective-permute-done.2 = bf16[2,32,2048]{2,1,0:T(8,128)(2,1)S(1)} collective-permute-done((bf16[2,32,2048]{2,1,0:T(8,128)(2,1)S(1)}, bf16[2,32,2048]{2,1,0:T(8,128)(2,1)S(1)}, u32[]{:S(2)}, u32[]{:S(2)}) %collective-permute-start.2) | collective-permute-done | bytes 262176 | tf_op jit(solution)/shard_map/ppermute | solution.py:17
  24.9 3.0 %add.316 = f32[8,4,128,16]{3,2,1,0:T(8,128)} reshape(f32[1,32,2048]{2,1,0:T(8,128)} %get-tuple-element.24) | data formatting | bytes 524288 | tf_op jit(solution)/shard_map/add | solution.py:44
  28.2 1.8 %reduce_sum.146 = f32[8,128]{1,0:T(8,128)S(1)} reduce(f32[8,4,128,16]{3,2,1,0:T(8,128)} %add.316, f32[]{:T(128)} %constant.95.clone.1), dimensions={1,3}, to_apply=%region_14.15 | reduce | flops 64512 | bytes 266244 | tf_op jit(solution)/shard_map/reduce_sum | solution.py:38
  45.9 1.9 %collective-permute-start.4 = (bf16[3,2,1,128]{3,1,2,0:T(2,128)(2,1)S(1)}, bf16[3,2,1,128]{3,1,2,0:T(2,128)(2,1)S(1)}, u32[]{:S(2)}, u32[]{:S(2)}) collective-permute-start(bf16[3,2,1,128]{3,1,2,0:T(2,128)(2,1)S(1)} %get-tuple-element.77), channel_id=1, source_target_pairs={{1,0},{2,1},{3,2},{5,4},{6,5},{7,6},{9,8},{10,9},{11,10},{13,12},{... | collective-permute-start | bytes 4616 | tf_op jit(solution)/shard_map/ppermute | solution.py:28
  47.9 2.4 %collective-permute-start.3 = (bf16[3,2,1,128]{3,1,2,0:T(2,128)(2,1)S(1)}, bf16[3,2,1,128]{3,1,2,0:T(2,128)(2,1)S(1)}, u32[]{:S(2)}, u32[]{:S(2)}) collective-permute-start(bf16[3,2,1,128]{3,1,2,0:T(2,128)(2,1)S(1)} %get-tuple-element.76), channel_id=1, source_target_pairs={{0,1},{1,2},{2,3},{4,5},{5,6},{6,7},{8,9},{9,10},{10,11},{12,13},{... | collective-permute-start | bytes 4616 | tf_op jit(solution)/shard_map/ppermute | solution.py:25
  50.5 2.3 %collective-permute-done.3 = bf16[3,2,1,128]{3,1,2,0:T(2,128)(2,1)S(1)} collective-permute-done((bf16[3,2,1,128]{3,1,2,0:T(2,128)(2,1)S(1)}, bf16[3,2,1,128]{3,1,2,0:T(2,128)(2,1)S(1)}, u32[]{:S(2)}, u32[]{:S(2)}) %collective-permute-start.3) | collective-permute-done | bytes 1568 | tf_op jit(solution)/shard_map/ppermute | solution.py:25
  53.0 4.2 %collective-permute-start.6 = (bf16[2,10,1]{2,0,1:T(2,128)(2,1)S(1)}, bf16[2,10,1]{2,0,1:T(2,128)(2,1)S(1)}, u32[]{:S(2)}, u32[]{:S(2)}) collective-permute-start(bf16[2,10,1]{2,0,1:T(2,128)(2,1)S(1)} %broadcast_select_fusion.29), channel_id=1, source_target_pairs={{0,8},{8,0},{4,12},{12,4},{16,24},{24,16},{20,28},{28,20},{1,9},{9... | collective-permute-start | bytes 128 | tf_op jit(solution)/shard_map/ppermute | solution.py:17
  59.0 1.9 %collective-permute-done.5 = bf16[2,10,1]{2,0,1:T(2,128)(2,1)S(1)} collective-permute-done((bf16[2,10,1]{2,0,1:T(2,128)(2,1)S(1)}, bf16[2,10,1]{2,0,1:T(2,128)(2,1)S(1)}, u32[]{:S(2)}, u32[]{:S(2)}) %collective-permute-start.5) | collective-permute-done | bytes 72 | tf_op jit(solution)/shard_map/ppermute | solution.py:17
  64.0 1.9 %collective-permute-start.9 = (bf16[3,64,1,128]{3,1,2,0:T(8,128)(2,1)S(1)}, bf16[3,64,1,128]{3,1,2,0:T(8,128)(2,1)S(1)}, u32[]{:S(2)}, u32[]{:S(2)}) collective-permute-start(bf16[3,64,1,128]{3,1,2,0:T(8,128)(2,1)S(1)} %get-tuple-element.52), channel_id=1, source_target_pairs={{1,0},{2,1},{3,2},{5,4},{6,5},{7,6},{9,8},{10,9},{11,10},{13,12},{... | collective-permute-start | bytes 147464 | tf_op jit(solution)/shard_map/ppermute | solution.py:28
  65.9 2.4 %collective-permute-start.8 = (bf16[3,64,1,128]{3,1,2,0:T(8,128)(2,1)S(1)}, bf16[3,64,1,128]{3,1,2,0:T(8,128)(2,1)S(1)}, u32[]{:S(2)}, u32[]{:S(2)}) collective-permute-start(bf16[3,64,1,128]{3,1,2,0:T(8,128)(2,1)S(1)} %get-tuple-element.51), channel_id=1, source_target_pairs={{0,1},{1,2},{2,3},{4,5},{5,6},{6,7},{8,9},{9,10},{10,11},{12,13},{... | collective-permute-start | bytes 147464 | tf_op jit(solution)/shard_map/ppermute | solution.py:25
  68.5 2.8 %collective-permute-done.8 = bf16[3,64,1,128]{3,1,2,0:T(8,128)(2,1)S(1)} collective-permute-done((bf16[3,64,1,128]{3,1,2,0:T(8,128)(2,1)S(1)}, bf16[3,64,1,128]{3,1,2,0:T(8,128)(2,1)S(1)}, u32[]{:S(2)}, u32[]{:S(2)}) %collective-permute-start.8) | collective-permute-done | bytes 49184 | tf_op jit(solution)/shard_map/ppermute | solution.py:25
  74.4 5.4 %collective-permute-done.12 = bf16[64,10,1]{2,0,1:T(8,128)(2,1)S(1)} collective-permute-done((bf16[64,10,1]{2,0,1:T(8,128)(2,1)S(1)}, bf16[64,10,1]{2,0,1:T(8,128)(2,1)S(1)}, u32[]{:S(2)}, u32[]{:S(2)}) %collective-permute-start.12) | collective-permute-done | bytes 1312 | tf_op jit(solution)/shard_map/ppermute | solution.py:17
  83.8 1.9 %collective-permute-start.14 = (bf16[3,64,1,128]{3,1,2,0:T(8,128)(2,1)S(1)}, bf16[3,64,1,128]{3,1,2,0:T(8,128)(2,1)S(1)}, u32[]{:S(2)}, u32[]{:S(2)}) collective-permute-start(bf16[3,64,1,128]{3,1,2,0:T(8,128)(2,1)S(1)} %get-tuple-element.50), channel_id=1, source_target_pairs={{1,0},{2,1},{3,2},{5,4},{6,5},{7,6},{9,8},{10,9},{11,10},{13,12},{... | collective-permute-start | bytes 147464 | tf_op jit(solution)/shard_map/ppermute | solution.py:28
  85.7 2.4 %collective-permute-start.13 = (bf16[3,64,1,128]{3,1,2,0:T(8,128)(2,1)S(1)}, bf16[3,64,1,128]{3,1,2,0:T(8,128)(2,1)S(1)}, u32[]{:S(2)}, u32[]{:S(2)}) collective-permute-start(bf16[3,64,1,128]{3,1,2,0:T(8,128)(2,1)S(1)} %get-tuple-element.49), channel_id=1, source_target_pairs={{0,1},{1,2},{2,3},{4,5},{5,6},{6,7},{8,9},{9,10},{10,11},{12,13},{... | collective-permute-start | bytes 147464 | tf_op jit(solution)/shard_map/ppermute | solution.py:25
  88.2 2.9 %collective-permute-done.13 = bf16[3,64,1,128]{3,1,2,0:T(8,128)(2,1)S(1)} collective-permute-done((bf16[3,64,1,128]{3,1,2,0:T(8,128)(2,1)S(1)}, bf16[3,64,1,128]{3,1,2,0:T(8,128)(2,1)S(1)}, u32[]{:S(2)}, u32[]{:S(2)}) %collective-permute-start.13) | collective-permute-done | bytes 49184 | tf_op jit(solution)/shard_map/ppermute | solution.py:25
  95.0 4.4 %collective-permute-done.17 = bf16[64,10,1]{2,0,1:T(8,128)(2,1)S(1)} collective-permute-done((bf16[64,10,1]{2,0,1:T(8,128)(2,1)S(1)}, bf16[64,10,1]{2,0,1:T(8,128)(2,1)S(1)}, u32[]{:S(2)}, u32[]{:S(2)}) %collective-permute-start.17) | collective-permute-done | bytes 1312 | tf_op jit(solution)/shard_map/ppermute | solution.py:17
  103.4 1.9 %collective-permute-start.19 = (bf16[3,64,1,128]{3,1,2,0:T(8,128)(2,1)S(1)}, bf16[3,64,1,128]{3,1,2,0:T(8,128)(2,1)S(1)}, u32[]{:S(2)}, u32[]{:S(2)}) collective-permute-start(bf16[3,64,1,128]{3,1,2,0:T(8,128)(2,1)S(1)} %get-tuple-element.48), channel_id=1, source_target_pairs={{1,0},{2,1},{3,2},{5,4},{6,5},{7,6},{9,8},{10,9},{11,10},{13,12},{... | collective-permute-start | bytes 147464 | tf_op jit(solution)/shard_map/ppermute | solution.py:28
  105.3 2.6 %collective-permute-start.18 = (bf16[3,64,1,128]{3,1,2,0:T(8,128)(2,1)S(1)}, bf16[3,64,1,128]{3,1,2,0:T(8,128)(2,1)S(1)}, u32[]{:S(2)}, u32[]{:S(2)}) collective-permute-start(bf16[3,64,1,128]{3,1,2,0:T(8,128)(2,1)S(1)} %get-tuple-element.47), channel_id=1, source_target_pairs={{0,1},{1,2},{2,3},{4,5},{5,6},{6,7},{8,9},{9,10},{10,11},{12,13},{... | collective-permute-start | bytes 147464 | tf_op jit(solution)/shard_map/ppermute | solution.py:25
  108.1 2.6 %collective-permute-done.18 = bf16[3,64,1,128]{3,1,2,0:T(8,128)(2,1)S(1)} collective-permute-done((bf16[3,64,1,128]{3,1,2,0:T(8,128)(2,1)S(1)}, bf16[3,64,1,128]{3,1,2,0:T(8,128)(2,1)S(1)}, u32[]{:S(2)}, u32[]{:S(2)}) %collective-permute-start.18) | collective-permute-done | bytes 49184 | tf_op jit(solution)/shard_map/ppermute | solution.py:25
  111.8 2.0 %collective-permute-start.21 = (bf16[64,10,1]{2,0,1:T(8,128)(2,1)S(1)}, bf16[64,10,1]{2,0,1:T(8,128)(2,1)S(1)}, u32[]{:S(2)}, u32[]{:S(2)}) collective-permute-start(bf16[64,10,1]{2,0,1:T(8,128)(2,1)S(1)} %slice_select_fusion.1), channel_id=1, source_target_pairs={{0,8},{8,0},{4,12},{12,4},{16,24},{24,16},{20,28},{28,20},{1,9},{9... | collective-permute-start | bytes 3848 | tf_op jit(solution)/shard_map/ppermute | solution.py:17
  115.5 3.9 %collective-permute-done.22 = bf16[64,10,1]{2,0,1:T(8,128)(2,1)S(1)} collective-permute-done((bf16[64,10,1]{2,0,1:T(8,128)(2,1)S(1)}, bf16[64,10,1]{2,0,1:T(8,128)(2,1)S(1)}, u32[]{:S(2)}, u32[]{:S(2)}) %collective-permute-start.22) | collective-permute-done | bytes 1312 | tf_op jit(solution)/shard_map/ppermute | solution.py:17
  122.7 30.7 %all_gather.3 = bf16[24,8,128]{2,1,0:T(8,128)(2,1)S(1)} all-gather(bf16[3,8,128]{2,1,0:T(8,128)(2,1)S(1)} %add_convert_fusion), channel_id=1, replica_groups=mesh['date'=8,'strip'=4] {'date'}, dimensions={0}, use_global_device_ids=true | all-gather | bytes 55296 | tf_op jit(solution)/shard_map/all_gather | solution.py:146
  (184 shorter events, 55.2 us)
Async XLA Ops:
  6.8 14.7 %collective-permute-start.2 = (bf16[2,32,2048]{2,1,0:T(8,128)(2,1)S(1)}, bf16[2,32,2048]{2,1,0:T(8,128)(2,1)S(1)}, u32[]{:S(2)}, u32[]{:S(2)}) collective-permute-start(bf16[2,32,2048]{2,1,0:T(8,128)(2,1)S(1)} %broadcast_select_fusion), channel_id=1, source_target_pairs={{0,16},{16,0},{4,20},{20,4},{8,24},{24,8},{12,28},{28,12},{1,17},{... | collective-permute-start | bytes 786440 | tf_op jit(solution)/shard_map/ppermute | solution.py:17
  10.2 22.6 %collective-permute-start = (bf16[2,32,2048]{2,1,0:T(8,128)(2,1)}, bf16[2,32,2048]{2,1,0:T(8,128)(2,1)}, u32[]{:S(2)}, u32[]{:S(2)}) collective-permute-start(bf16[2,32,2048]{2,1,0:T(8,128)(2,1)} %broadcast_select_fusion.4), channel_id=1, source_target_pairs={{0,4},{4,0},{8,12},{12,8},{16,20},{20,16},{24,28},{28,24},{1,5},{5... | collective-permute-start | bytes 786440 | tf_op jit(solution)/shard_map/ppermute | solution.py:17
  12.5 27.6 %collective-permute-start.1 = (bf16[2,32,2048]{2,1,0:T(8,128)(2,1)}, bf16[2,32,2048]{2,1,0:T(8,128)(2,1)}, u32[]{:S(2)}, u32[]{:S(2)}) collective-permute-start(bf16[2,32,2048]{2,1,0:T(8,128)(2,1)} %broadcast_select_fusion.2), channel_id=1, source_target_pairs={{0,8},{8,0},{4,12},{12,4},{16,24},{24,16},{20,28},{28,20},{1,9},{9... | collective-permute-start | bytes 786440 | tf_op jit(solution)/shard_map/ppermute | solution.py:17
  45.9 4.5 %collective-permute-start.4 = (bf16[3,2,1,128]{3,1,2,0:T(2,128)(2,1)S(1)}, bf16[3,2,1,128]{3,1,2,0:T(2,128)(2,1)S(1)}, u32[]{:S(2)}, u32[]{:S(2)}) collective-permute-start(bf16[3,2,1,128]{3,1,2,0:T(2,128)(2,1)S(1)} %get-tuple-element.77), channel_id=1, source_target_pairs={{1,0},{2,1},{3,2},{5,4},{6,5},{7,6},{9,8},{10,9},{11,10},{13,12},{... | collective-permute-start | bytes 4616 | tf_op jit(solution)/shard_map/ppermute | solution.py:28
  47.9 4.9 %collective-permute-start.3 = (bf16[3,2,1,128]{3,1,2,0:T(2,128)(2,1)S(1)}, bf16[3,2,1,128]{3,1,2,0:T(2,128)(2,1)S(1)}, u32[]{:S(2)}, u32[]{:S(2)}) collective-permute-start(bf16[3,2,1,128]{3,1,2,0:T(2,128)(2,1)S(1)} %get-tuple-element.76), channel_id=1, source_target_pairs={{0,1},{1,2},{2,3},{4,5},{5,6},{6,7},{8,9},{9,10},{10,11},{12,13},{... | collective-permute-start | bytes 4616 | tf_op jit(solution)/shard_map/ppermute | solution.py:25
  52.9 5.9 %collective-permute-start.7 = (bf16[2,10,1]{2,0,1:T(2,128)(2,1)S(1)}, bf16[2,10,1]{2,0,1:T(2,128)(2,1)S(1)}, u32[]{:S(2)}, u32[]{:S(2)}) collective-permute-start(bf16[2,10,1]{2,0,1:T(2,128)(2,1)S(1)} %broadcast_select_fusion.26), channel_id=1, source_target_pairs={{0,16},{16,0},{4,20},{20,4},{8,24},{24,8},{12,28},{28,12},{1,17},{... | collective-permute-start | bytes 128 | tf_op jit(solution)/shard_map/ppermute | solution.py:17
  53.0 5.9 %collective-permute-start.6 = (bf16[2,10,1]{2,0,1:T(2,128)(2,1)S(1)}, bf16[2,10,1]{2,0,1:T(2,128)(2,1)S(1)}, u32[]{:S(2)}, u32[]{:S(2)}) collective-permute-start(bf16[2,10,1]{2,0,1:T(2,128)(2,1)S(1)} %broadcast_select_fusion.29), channel_id=1, source_target_pairs={{0,8},{8,0},{4,12},{12,4},{16,24},{24,16},{20,28},{28,20},{1,9},{9... | collective-permute-start | bytes 128 | tf_op jit(solution)/shard_map/ppermute | solution.py:17
  57.3 3.6 %collective-permute-start.5 = (bf16[2,10,1]{2,0,1:T(2,128)(2,1)S(1)}, bf16[2,10,1]{2,0,1:T(2,128)(2,1)S(1)}, u32[]{:S(2)}, u32[]{:S(2)}) collective-permute-start(bf16[2,10,1]{2,0,1:T(2,128)(2,1)S(1)} %broadcast_select_fusion.32), channel_id=1, source_target_pairs={{0,4},{4,0},{8,12},{12,8},{16,20},{20,16},{24,28},{28,24},{1,5},{5... | collective-permute-start | bytes 128 | tf_op jit(solution)/shard_map/ppermute | solution.py:17
  64.0 4.5 %collective-permute-start.9 = (bf16[3,64,1,128]{3,1,2,0:T(8,128)(2,1)S(1)}, bf16[3,64,1,128]{3,1,2,0:T(8,128)(2,1)S(1)}, u32[]{:S(2)}, u32[]{:S(2)}) collective-permute-start(bf16[3,64,1,128]{3,1,2,0:T(8,128)(2,1)S(1)} %get-tuple-element.52), channel_id=1, source_target_pairs={{1,0},{2,1},{3,2},{5,4},{6,5},{7,6},{9,8},{10,9},{11,10},{13,12},{... | collective-permute-start | bytes 147464 | tf_op jit(solution)/shard_map/ppermute | solution.py:28
  65.9 5.4 %collective-permute-start.8 = (bf16[3,64,1,128]{3,1,2,0:T(8,128)(2,1)S(1)}, bf16[3,64,1,128]{3,1,2,0:T(8,128)(2,1)S(1)}, u32[]{:S(2)}, u32[]{:S(2)}) collective-permute-start(bf16[3,64,1,128]{3,1,2,0:T(8,128)(2,1)S(1)} %get-tuple-element.51), channel_id=1, source_target_pairs={{0,1},{1,2},{2,3},{4,5},{5,6},{6,7},{8,9},{9,10},{10,11},{12,13},{... | collective-permute-start | bytes 147464 | tf_op jit(solution)/shard_map/ppermute | solution.py:25
  71.5 8.2 %collective-permute-start.12 = (bf16[64,10,1]{2,0,1:T(8,128)(2,1)S(1)}, bf16[64,10,1]{2,0,1:T(8,128)(2,1)S(1)}, u32[]{:S(2)}, u32[]{:S(2)}) collective-permute-start(bf16[64,10,1]{2,0,1:T(8,128)(2,1)S(1)} %slice_select_fusion.6), channel_id=1, source_target_pairs={{0,16},{16,0},{4,20},{20,4},{8,24},{24,8},{12,28},{28,12},{1,17},{... | collective-permute-start | bytes 3848 | tf_op jit(solution)/shard_map/ppermute | solution.py:17
  71.7 8.3 %collective-permute-start.11 = (bf16[64,10,1]{2,0,1:T(8,128)(2,1)S(1)}, bf16[64,10,1]{2,0,1:T(8,128)(2,1)S(1)}, u32[]{:S(2)}, u32[]{:S(2)}) collective-permute-start(bf16[64,10,1]{2,0,1:T(8,128)(2,1)S(1)} %slice_select_fusion.7), channel_id=1, source_target_pairs={{0,8},{8,0},{4,12},{12,4},{16,24},{24,16},{20,28},{28,20},{1,9},{9... | collective-permute-start | bytes 3848 | tf_op jit(solution)/shard_map/ppermute | solution.py:17
  72.8 7.5 %collective-permute-start.10 = (bf16[64,10,1]{2,0,1:T(8,128)(2,1)S(1)}, bf16[64,10,1]{2,0,1:T(8,128)(2,1)S(1)}, u32[]{:S(2)}, u32[]{:S(2)}) collective-permute-start(bf16[64,10,1]{2,0,1:T(8,128)(2,1)S(1)} %slice_select_fusion.8), channel_id=1, source_target_pairs={{0,4},{4,0},{8,12},{12,8},{16,20},{20,16},{24,28},{28,24},{1,5},{5... | collective-permute-start | bytes 3848 | tf_op jit(solution)/shard_map/ppermute | solution.py:17
  83.8 4.5 %collective-permute-start.14 = (bf16[3,64,1,128]{3,1,2,0:T(8,128)(2,1)S(1)}, bf16[3,64,1,128]{3,1,2,0:T(8,128)(2,1)S(1)}, u32[]{:S(2)}, u32[]{:S(2)}) collective-permute-start(bf16[3,64,1,128]{3,1,2,0:T(8,128)(2,1)S(1)} %get-tuple-element.50), channel_id=1, source_target_pairs={{1,0},{2,1},{3,2},{5,4},{6,5},{7,6},{9,8},{10,9},{11,10},{13,12},{... | collective-permute-start | bytes 147464 | tf_op jit(solution)/shard_map/ppermute | solution.py:28
  85.7 5.4 %collective-permute-start.13 = (bf16[3,64,1,128]{3,1,2,0:T(8,128)(2,1)S(1)}, bf16[3,64,1,128]{3,1,2,0:T(8,128)(2,1)S(1)}, u32[]{:S(2)}, u32[]{:S(2)}) collective-permute-start(bf16[3,64,1,128]{3,1,2,0:T(8,128)(2,1)S(1)} %get-tuple-element.49), channel_id=1, source_target_pairs={{0,1},{1,2},{2,3},{4,5},{5,6},{6,7},{8,9},{9,10},{10,11},{12,13},{... | collective-permute-start | bytes 147464 | tf_op jit(solution)/shard_map/ppermute | solution.py:25
  91.3 8.0 %collective-permute-start.17 = (bf16[64,10,1]{2,0,1:T(8,128)(2,1)S(1)}, bf16[64,10,1]{2,0,1:T(8,128)(2,1)S(1)}, u32[]{:S(2)}, u32[]{:S(2)}) collective-permute-start(bf16[64,10,1]{2,0,1:T(8,128)(2,1)S(1)} %slice_select_fusion.3), channel_id=1, source_target_pairs={{0,16},{16,0},{4,20},{20,4},{8,24},{24,8},{12,28},{28,12},{1,17},{... | collective-permute-start | bytes 3848 | tf_op jit(solution)/shard_map/ppermute | solution.py:17
  92.0 7.7 %collective-permute-start.16 = (bf16[64,10,1]{2,0,1:T(8,128)(2,1)S(1)}, bf16[64,10,1]{2,0,1:T(8,128)(2,1)S(1)}, u32[]{:S(2)}, u32[]{:S(2)}) collective-permute-start(bf16[64,10,1]{2,0,1:T(8,128)(2,1)S(1)} %slice_select_fusion.4), channel_id=1, source_target_pairs={{0,8},{8,0},{4,12},{12,4},{16,24},{24,16},{20,28},{28,20},{1,9},{9... | collective-permute-start | bytes 3848 | tf_op jit(solution)/shard_map/ppermute | solution.py:17
  93.4 6.5 %collective-permute-start.15 = (bf16[64,10,1]{2,0,1:T(8,128)(2,1)S(1)}, bf16[64,10,1]{2,0,1:T(8,128)(2,1)S(1)}, u32[]{:S(2)}, u32[]{:S(2)}) collective-permute-start(bf16[64,10,1]{2,0,1:T(8,128)(2,1)S(1)} %slice_select_fusion.5), channel_id=1, source_target_pairs={{0,4},{4,0},{8,12},{12,8},{16,20},{20,16},{24,28},{28,24},{1,5},{5... | collective-permute-start | bytes 3848 | tf_op jit(solution)/shard_map/ppermute | solution.py:17
  103.4 4.7 %collective-permute-start.19 = (bf16[3,64,1,128]{3,1,2,0:T(8,128)(2,1)S(1)}, bf16[3,64,1,128]{3,1,2,0:T(8,128)(2,1)S(1)}, u32[]{:S(2)}, u32[]{:S(2)}) collective-permute-start(bf16[3,64,1,128]{3,1,2,0:T(8,128)(2,1)S(1)} %get-tuple-element.48), channel_id=1, source_target_pairs={{1,0},{2,1},{3,2},{5,4},{6,5},{7,6},{9,8},{10,9},{11,10},{13,12},{... | collective-permute-start | bytes 147464 | tf_op jit(solution)/shard_map/ppermute | solution.py:28
  105.3 5.4 %collective-permute-start.18 = (bf16[3,64,1,128]{3,1,2,0:T(8,128)(2,1)S(1)}, bf16[3,64,1,128]{3,1,2,0:T(8,128)(2,1)S(1)}, u32[]{:S(2)}, u32[]{:S(2)}) collective-permute-start(bf16[3,64,1,128]{3,1,2,0:T(8,128)(2,1)S(1)} %get-tuple-element.47), channel_id=1, source_target_pairs={{0,1},{1,2},{2,3},{4,5},{5,6},{6,7},{8,9},{9,10},{10,11},{12,13},{... | collective-permute-start | bytes 147464 | tf_op jit(solution)/shard_map/ppermute | solution.py:25
  110.9 8.4 %collective-permute-start.22 = (bf16[64,10,1]{2,0,1:T(8,128)(2,1)S(1)}, bf16[64,10,1]{2,0,1:T(8,128)(2,1)S(1)}, u32[]{:S(2)}, u32[]{:S(2)}) collective-permute-start(bf16[64,10,1]{2,0,1:T(8,128)(2,1)S(1)} %slice_select_fusion), channel_id=1, source_target_pairs={{0,16},{16,0},{4,20},{20,4},{8,24},{24,8},{12,28},{28,12},{1,17},{... | collective-permute-start | bytes 3848 | tf_op jit(solution)/shard_map/ppermute | solution.py:17
  111.8 7.9 %collective-permute-start.21 = (bf16[64,10,1]{2,0,1:T(8,128)(2,1)S(1)}, bf16[64,10,1]{2,0,1:T(8,128)(2,1)S(1)}, u32[]{:S(2)}, u32[]{:S(2)}) collective-permute-start(bf16[64,10,1]{2,0,1:T(8,128)(2,1)S(1)} %slice_select_fusion.1), channel_id=1, source_target_pairs={{0,8},{8,0},{4,12},{12,4},{16,24},{24,16},{20,28},{28,20},{1,9},{9... | collective-permute-start | bytes 3848 | tf_op jit(solution)/shard_map/ppermute | solution.py:17
  113.9 6.0 %collective-permute-start.20 = (bf16[64,10,1]{2,0,1:T(8,128)(2,1)S(1)}, bf16[64,10,1]{2,0,1:T(8,128)(2,1)S(1)}, u32[]{:S(2)}, u32[]{:S(2)}) collective-permute-start(bf16[64,10,1]{2,0,1:T(8,128)(2,1)S(1)} %slice_select_fusion.2), channel_id=1, source_target_pairs={{0,4},{4,0},{8,12},{12,8},{16,20},{20,16},{24,28},{28,24},{1,5},{5... | collective-permute-start | bytes 3848 | tf_op jit(solution)/shard_map/ppermute | solution.py:17
  120.4 33.9 %copy-start.1 = (f32[16,12]{1,0:T(8,128)S(1)}, f32[16,12]{1,0:T(8,128)}, u32[]{:S(2)}) copy-start(f32[16,12]{1,0:T(8,128)} %param.11) | copy-start | bytes 2308
  (6 other events, 42.8 us)
where the time goes:
time: 155 us; the launch traced here: 154 us
  starting transfers between devices  39.6 us (26%)
  waiting for transfers between devices  32.4 us (21%)
  blocking collectives  30.7 us (20%)
  other arithmetic  20.2 us (13%)
  local copies, waits for them, and re-layouts  17.3 us (11%)
  matrix products  11.1 us (7%)
  between operations  2.92 us (2%)
    all_gather x1, blocking collectives, per_device(): lax.all_gather(phases, 'date', axis=0, tiled=True).astype(jnp.float32)  30.7 us
    ppermute x15, starting transfers between devices, from_partner(): return lax.ppermute(block, axis, route)  22 us
    ppermute x15, waiting for transfers between devices, from_partner(): return lax.ppermute(block, axis, route)  21.9 us
    ppermute x4, waiting for transfers between devices, extended_2(): lax.ppermute(lax.slice_in_dim(block, block.shape[dim] - width, None, axis...  10.6 us
    dot_general x36, matrix products, convolve(): jnp.einsum('oi,pirc->porc', weight[tap_row, tap_col], piece, preferred_el...  10.4 us
    ppermute x4, starting transfers between devices, extended_2(): lax.ppermute(lax.slice_in_dim(block, block.shape[dim] - width, None, axis...  9.84 us
    ppermute x4, starting transfers between devices, extended_2(): lax.ppermute(lax.slice_in_dim(block, 0, width, axis=dim), axis, backward)  7.68 us
    add x3, local copies, waits for them, and re-layouts, coherence_of(): real_part = first[0] * second[0] + first[1] * second[1]  4.44 us
  transfers between devices with their start and end apart: 23, of which 9 were waited for; matrix products, arithmetic and copies ran while one was open for 16% of the time, Pallas kernels for 0%

commit v1 on v0

v1 whole, which is shorter than its diff:
```python
import functools

import jax
import jax.numpy as jnp
from jax import lax
from jax.experimental import pallas as pl
from jax.experimental.pallas import tpu as pltpu
from jax.sharding import PartitionSpec as P

LOOK_R = 4
LOOK_C = 16
WIN = 144
EDGE = 8
NT = (((1,), (1,)), ((), ()))
TN = (((0,), (0,)), ((), ()))
MESH = pl.DeviceIdType.MESH
F32 = jnp.float32
BF16 = jnp.bfloat16


def iota(shape, dim):
    return lax.broadcasted_iota(jnp.int32, shape, dim)


def third(value):
    return (value * 11) >> 5


def flag(cond):
    return jnp.where(cond, 1.0, 0.0)


def kernel(
    n_date,
    n_strip,
    scenes,
    pairs,
    inversion,
    w_first,
    w_mid,
    w_last,
    out,
    tile,
    sendbuf,
    recvbuf,
    select,
    prods,
    sums,
    xs,
    base_first,
    big_first,
    big_mid,
    rows_last,
    big_last,
    col_mask,
    hid_a,
    hid_b,
    hid_c,
    last_out,
    gathered,
    load_sem,
    ex_send,
    ex_recv,
    halo_send,
    halo_recv,
    ga_send,
    ga_recv,
):
    me = lax.axis_index("date")
    strip = lax.axis_index("strip")
    date_dev = scenes.shape[1]
    cols = scenes.shape[3]
    span = sendbuf.shape[-1]
    block = n_date // 2
    bits = [0, 1, n_date.bit_length() - 2]
    total_rows = n_strip * 8

    barrier = pltpu.get_barrier_semaphore()

    def greet(j, carry):
        pl.semaphore_signal(
            barrier, inc=1, device_id=(lax.rem(me + j, n_date), strip), device_id_type=MESH
        )
        return carry

    lax.fori_loop(1, n_date, greet, 0)

    @pl.when(strip > 0)
    def _():
        pl.semaphore_signal(barrier, inc=1, device_id=(me, strip - 1), device_id_type=MESH)

    @pl.when(strip < n_strip - 1)
    def _():
        pl.semaphore_signal(barrier, inc=1, device_id=(me, strip + 1), device_id_type=MESH)

    load = pltpu.make_async_copy(scenes, tile, load_sem)
    load.start()

    upper, partner, own_date, sign = [], [], [], []
    for m in range(3):
        step = 1 << bits[m]
        side = lax.rem(me // step, 2)
        upper.append(side)
        partner.append(me + step - 2 * step * side)

        def pick(i, carry, m=m):
            date, is_ref = carry
            ref = pairs[m * block + i, 0]
            sec = pairs[m * block + i, 1]
            ref_hit = ref // date_dev == me
            sec_hit = sec // date_dev == me
            date = jnp.where(ref_hit, ref, jnp.where(sec_hit, sec, date))
            return date, jnp.where(ref_hit, 1, is_ref)

        date, is_ref = lax.fori_loop(
            0, block, pick, (me * date_dev, jnp.int32(0)), unroll=block <= 8
        )
        own_date.append(date - me * date_dev)
        sign.append(jnp.where(is_ref == 1, 1.0, -1.0).astype(F32))

    load.wait()
    pl.semaphore_wait(
        barrier,
        n_date - 1 + jnp.where(strip > 0, 1, 0) + jnp.where(strip < n_strip - 1, 1, 0),
    )

    exchange = {}
    for m in (2, 0, 1):
        offset = pl.multiple_of((1 - upper[m]) * (cols - span), 128)
        for h in range(2):
            for c in range(2):
                sendbuf[m, h, c] = tile[c, own_date[m], h * 16 : h * 16 + 16, pl.ds(offset, span)]
            exchange[m, h] = pltpu.make_async_remote_copy(
                src_ref=sendbuf.at[m, h],
                dst_ref=recvbuf.at[m, h],
                send_sem=ex_send.at[m, h],
                recv_sem=ex_recv.at[m, h],
                device_id=(partner[m], strip),
                device_id_type=MESH,
            )
            exchange[m, h].start()

    def fill_select(j, carry):
        apart = iota((128, 256), 0) + j * 128 - LOOK_C * iota((128, 256), 1)
        rows = pl.ds(pl.multiple_of(j * 128, 128), 128)
        select[rows, :] = flag((apart >= 0) & (apart < LOOK_C)).astype(BF16)
        return carry

    lax.fori_loop(0, span // 128, fill_select, 0)

    base_first[...] = jnp.zeros_like(base_first)
    nothing = jnp.zeros((64, 2), BF16)
    eye_small = flag(iota((8, 2), 0) == iota((8, 2), 1)).astype(BF16)
    for b in range(4):
        for q in range(3):
            stack = jnp.concatenate(
                [w_first[b, q] if b < 3 else nothing, w_first[b - 1, q] if b > 0 else nothing],
                axis=0,
            )
            turned = lax.dot_general(eye_small, stack, NT, preferred_element_type=F32)
            place = (b * 3 + q) * 2
            base_first[place : place + 2, :] = turned[:2]
    base = base_first[...].astype(BF16)
    k = iota((96, 32), 0)
    n = iota((96, 32), 1)
    same = ((k >> 5) == (n >> 1) - 3 * third(n >> 1)) & (((k >> 2) & 1) == (n & 1))
    row = ((k >> 3) & 3) * 4 + (k & 3) - third(n >> 1)
    for i in range(7):
        pickrow = flag(same & (row == 2 * i)).astype(BF16)
        big_first[:, i * 128 : i * 128 + 128] = jnp.dot(
            pickrow, base, preferred_element_type=F32
        ).astype(BF16)

    blank = jnp.zeros((64, 64), BF16)
    eye = flag(iota((64, 64), 0) == iota((64, 64), 1)).astype(BF16)
    for layer in range(2):
        for b in range(4):
            for q in range(3):
                stack = jnp.concatenate(
                    [
                        w_mid[layer, b, q] if b < 3 else blank,
                        w_mid[layer, b - 1, q] if b > 0 else blank,
                    ],
                    axis=0,
                )
                turned = lax.dot_general(eye, stack, NT, preferred_element_type=F32)
                place = (b // 2) * 384 + q * 128 + (b % 2) * 64
                big_mid[layer, place : place + 64, :] = turned.astype(BF16)

    rows_last[...] = jnp.zeros_like(rows_last)
    for p in range(3):
        for q in range(3):
            rows_last[p * 3 + q : p * 3 + q + 1, :] = w_last[p, q].astype(F32)
    twice = flag((iota((64, 128), 1) & 63) == iota((64, 128), 0)).astype(BF16)
    both = jnp.dot(rows_last[...].astype(BF16), twice, preferred_element_type=F32).astype(BF16)
    k = iota((24, 16), 0)
    n = iota((24, 16), 1)
    same = (k >> 3) == n - 3 * third(n)
    tap = third(n) + (k & 7)
    first_half = iota((24, 128), 1) < 64
    for i in range(5):
        parts = [
            jnp.dot(
                flag(same & (tap == 2 * i + a)).astype(BF16), both, preferred_element_type=F32
            )
            for a in range(2)
        ]
        big_last[:, i * 128 : i * 128 + 128] = jnp.where(first_half, parts[0], parts[1]).astype(
            BF16
        )

    last_out[...] = jnp.zeros_like(last_out)
    window = iota((WIN, 128), 0)
    for m in range(3):
        low = EDGE * (1 - upper[m])
        col_mask[m] = flag((window >= low) & (window < WIN - EDGE + low))

    @pl.when(strip == 0)
    def _():
        xs[:, 0:8, :] = jnp.zeros((3, 8, 256), F32)

    @pl.when(strip == n_strip - 1)
    def _():
        xs[:, 24:32, :] = jnp.zeros((3, 8, 256), F32)

    def halo(m, side):
        source = 8 if side == 0 else 16
        target = 24 if side == 0 else 0
        return pltpu.make_async_remote_copy(
            src_ref=xs.at[m, source : source + 8],
            dst_ref=xs.at[m, target : target + 8],
            send_sem=halo_send.at[m, side],
            recv_sem=halo_recv.at[m, side],
            device_id=(me, strip - 1 if side == 0 else strip + 1),
            device_id_type=MESH,
        )

    def look(m, h):
        own_offset = pl.multiple_of(upper[m] * (cols - span), 128)

        def columns(start, width):
            rows = slice(h * 16, h * 16 + 16)
            own = pl.ds(pl.multiple_of(own_offset + start, 128), width)
            there = pl.ds(start, width)
            a0 = tile[0, own_date[m], rows, own].astype(F32)
            a1 = tile[1, own_date[m], rows, own].astype(F32)
            b0 = recvbuf[m, h, 0, :, there].astype(F32)
            b1 = recvbuf[m, h, 1, :, there].astype(F32)
            fields = (
                a0 * b0 + a1 * b1,
                a1 * b0 - a0 * b1,
                a0 * a0 + a1 * a1,
                b0 * b0 + b1 * b1,
            )
            for f, field in enumerate(fields):
                high = field.astype(BF16)
                prods[f * 16 : f * 16 + 16, there] = high
                prods[64 + f * 16 : 80 + f * 16, there] = (field - high.astype(F32)).astype(BF16)

        def step(j, carry):
            columns(pl.multiple_of(j * 256, 256), 256)
            return carry

        lax.fori_loop(0, span // 256, step, 0, unroll=2)
        columns(span // 256 * 256, span % 256)
        looked = jnp.dot(prods[...], select[...], preferred_element_type=F32)
        looked = looked[:64] + looked[64:]
        sums[0] = looked[:, :128]
        sums[1] = looked[:, 128:]
        halves = []
        for part in range(2):
            total = sums[part, pl.ds(0, 16, stride=4), :]
            for r in range(1, 4):
                total = total + sums[part, pl.ds(r, 16, stride=4), :]
            powers = total[8:]
            powers = powers * pltpu.roll(powers, 4, 0)
            signed = total[:8] * jnp.where(iota((8, 128), 0) < 4, 1.0, sign[m])
            halves.append((signed * lax.rsqrt(powers + 1e-06)).astype(BF16).astype(F32))
        slab = jnp.concatenate(halves, axis=1)
        slab = pltpu.roll(slab, EDGE * (1 - upper[m]), 1)
        xs[m, 8 + h * 8 : 16 + h * 8, :] = slab

        @pl.when(strip > 0 if h == 0 else strip < n_strip - 1)
        def _():
            halo(m, h).start()

    def spread(target, i, value):
        value_rows = slice(i * WIN, i * WIN + WIN)
        target[value_rows, 0:128] = pltpu.roll(value, 1, 0).astype(BF16)
        target[value_rows, 128:256] = value.astype(BF16)
        target[value_rows, 256:384] = pltpu.roll(value, WIN - 1, 0).astype(BF16)

    def masked(m, value, i, first_row):
        value = jnp.maximum(value, 0.0) * col_mask[m]
        low = first_row + 2 * i
        if low < 0 or low + 1 > 7:
            rows = strip * 8 + low + (iota((1, 128), 1) >> 6)
            value = value * flag((rows >= 0) & (rows < total_rows))
        return value

    def peer_copy(m, j):
        return pltpu.make_async_remote_copy(
            src_ref=gathered.at[m, me],
            dst_ref=gathered.at[m, me],
            send_sem=ga_send.at[m, j],
            recv_sem=ga_recv.at[m, j],
            device_id=(lax.rem(me + j, n_date), strip),
            device_id_type=MESH,
        )

    def network(m):
        @pl.when(strip > 0)
        def _():
            halo(m, 1).wait_recv()

        @pl.when(strip < n_strip - 1)
        def _():
            halo(m, 0).wait_recv()

        x = xs[m]
        x = jnp.concatenate([pltpu.roll(x, 1, 1), x, pltpu.roll(x, 255, 1)], axis=0)
        x = x.astype(BF16)
        wide = lax.dot_general(x, big_first[...], TN, preferred_element_type=F32)[:WIN]
        for i in range(7):
            spread(hid_a, i, masked(m, wide[:, i * 128 : i * 128 + 128], i, -3))
        for layer, (source, count) in enumerate(((hid_a, 6), (hid_b, 5))):
            size = count * WIN
            patches = jnp.concatenate([source[:size, :], source[WIN : WIN + size, :]], axis=1)
            wide = jnp.dot(patches, big_mid[layer], preferred_element_type=F32)
            for i in range(count):
                value = masked(m, wide[i * WIN : i * WIN + WIN], i, layer - 2)
                if layer == 0:
                    spread(hid_b, i, value)
                else:
                    hid_c[:, i * 128 : i * 128 + 128] = value.astype(BF16)
        last_out[:, :WIN] = lax.dot_general(
            big_last[...], hid_c[...], NT, preferred_element_type=F32
        )
        phase = (
            pltpu.roll(last_out[0:8], 256 - (EDGE - 1), 1)
            + pltpu.roll(last_out[8:16], 256 - EDGE, 1)
            + pltpu.roll(last_out[16:24], 256 - (EDGE + 1), 1)
        )[:, :128]
        gathered[m, me] = phase.astype(BF16).astype(F32)

        def tell(j, carry):
            peer_copy(m, j).start()
            return carry

        lax.fori_loop(1, n_date, tell, 0)

    for m in (0, 1):
        for h in range(2):
            exchange[m, h].wait_recv()
            look(m, h)
    network(0)
    network(1)
    for h in range(2):
        exchange[2, h].wait_recv()
        look(2, h)
    network(2)

    for m in range(3):
        for h in range(2):
            exchange[m, h].wait_send()

            @pl.when(strip > 0 if h == 0 else strip < n_strip - 1)
            def _(m=m, h=h):
                halo(m, h).wait_send()

        def hear(j, carry, m=m):
            copy = peer_copy(m, j)
            copy.wait_send()
            copy.wait_recv()
            return carry

        lax.fori_loop(1, n_date, hear, 0)

    zero = jnp.zeros((8, 128), F32)
    acc = (zero,) * (2 * date_dev)
    for m in range(3):

        def add(i, acc, m=m):
            pair = m * block + i
            ref = pairs[pair, 0] // date_dev
            sec = pairs[pair, 1] // date_dev
            left = gathered[m, jnp.minimum(ref, sec)]
            right = gathered[m, jnp.maximum(ref, sec)]
            result = []
            for t in range(date_dev):
                gain = inversion[me * date_dev + t, pair]
                result += [acc[2 * t] + gain * left, acc[2 * t + 1] + gain * right]
            return tuple(result)

        acc = lax.fori_loop(0, block, add, acc, unroll=block <= 8)
    for t in range(date_dev):
        out[t, :, 0:128] = acc[2 * t]
        out[t, :, 128:256] = acc[2 * t + 1]


def per_device(scenes, date_pairs, first_weight, mid_weight, last_weight, inversion):
    n_date = lax.axis_size("date")
    n_strip = lax.axis_size("strip")
    date_dev = scenes.shape[1]
    cols = scenes.shape[3]
    span = cols // 2 + EDGE * LOOK_C
    vmem = pl.BlockSpec(memory_space=pltpu.VMEM)
    smem = pl.BlockSpec(memory_space=pltpu.SMEM)
    dma = pltpu.SemaphoreType.DMA
    return pl.pallas_call(
        functools.partial(kernel, n_date, n_strip),
        out_shape=jax.ShapeDtypeStruct((date_dev, 8, 256), F32),
        in_specs=[pl.BlockSpec(memory_space=pl.ANY), smem, smem, vmem, vmem, vmem],
        out_specs=vmem,
        scratch_shapes=[
            pltpu.VMEM(scenes.shape, BF16),
            pltpu.VMEM((3, 2, 2, 16, span), BF16),
            pltpu.VMEM((3, 2, 2, 16, span), BF16),
            pltpu.VMEM((span, 256), BF16),
            pltpu.VMEM((128, span), BF16),
            pltpu.VMEM((2, 64, 128), F32),
            pltpu.VMEM((3, 32, 256), F32),
            pltpu.VMEM((32, 128), F32),
            pltpu.VMEM((96, 7 * 128), BF16),
            pltpu.VMEM((2, 768, 128), BF16),
            pltpu.VMEM((16, 64), F32),
            pltpu.VMEM((24, 5 * 128), BF16),
            pltpu.VMEM((3, WIN, 128), F32),
            pltpu.VMEM((7 * WIN, 384), BF16),
            pltpu.VMEM((6 * WIN, 384), BF16),
            pltpu.VMEM((WIN, 5 * 128), BF16),
            pltpu.VMEM((24, 256), F32),
            pltpu.VMEM((3, n_date, 8, 128), F32),
            dma,
            dma((3, 2)),
            dma((3, 2)),
            dma((3, 2)),
            dma((3, 2)),
            dma((3, n_date)),
            dma((3, n_date)),
        ],
        compiler_params=pltpu.CompilerParams(
            collective_id=0, has_side_effects=True, vmem_limit_bytes=40 * 1024 * 1024
        ),
    )(scenes, date_pairs, inversion, first_weight, mid_weight, last_weight)


def solution(mesh):
    return jax.shard_map(
        per_device,
        mesh=mesh,
        in_specs=(P(None, "date", "strip", None), P(), P(), P(), P(), P()),
        out_specs=P("date", "strip", None),
        check_vma=False,
    )
```

time: 155 us -> 37.8 us (0.24)
  the two profiles are of different devices: /device:TPU:2 before, /device:TPU:1 now
where the time goes in v1:
time: 37.8 us; the launch traced here: 37.5 us
  Pallas kernels  32.6 us (86%)
  local copies, waits for them, and re-layouts  4.88 us (13%)
    pallas_call x1, Pallas kernels, per_device(): pl.pallas_call(functools.partial(kernel, n_date, n_strip), out_shape=jax....  32.6 us
    unnamed x14, local copies, waits for them, and re-layouts  4.88 us

profile of v1, /device:TPU:1, one launch (start us, length us, event | category | flops | bytes accessed | tf_op | source)
XLA Modules:
  0.0 37.5 jit_solution(12386659123162766919)
XLA Ops:
  0.0 0.0 copy-start.4
  0.0 0.7 %copy.9.w_last = bf16[3,3,1,64]{3,2,1,0:T(2,128)(2,1)S(1)} copy(bf16[3,3,1,64]{3,1,2,0:T(4,128)(2,1)} %param.10) | data formatting | bytes 2304 | tf_op args[4]
  0.7 0.0 copy-done.4
  0.7 0.0 copy-start.3
  0.7 0.1 copy.7.pairs
  0.8 0.6 %copy-done.3 = bf16[3,3,64,2]{2,3,1,0:T(2,128)(2,1)S(1)} copy-done((bf16[3,3,64,2]{2,3,1,0:T(2,128)(2,1)S(1)}, bf16[3,3,64,2]{2,3,1,0:T(2,128)(2,1)}, u32[]{:S(2)}) %copy-start.3) | copy-done | bytes 2328
  1.4 0.0 copy-start.2
  1.4 0.2 copy.8.w_first
  1.6 0.5 %copy-done.2 = f32[16,12]{1,0:T(8,128)S(1)} copy-done((f32[16,12]{1,0:T(8,128)S(1)}, f32[16,12]{1,0:T(8,128)}, u32[]{:S(2)}) %copy-start.2) | copy-done | bytes 792
  2.1 0.0 copy-start
  2.1 1.2 %copy-done = bf16[2,2,32,4096]{3,2,1,0:T(8,128)(2,1)S(1)} copy-done((bf16[2,2,32,4096]{3,2,1,0:T(8,128)(2,1)S(1)}, bf16[2,2,32,4096]{3,2,1,0:T(8,128)(2,1)}, u32[]{:S(2)}) %copy-start) | copy-done | bytes 1048600
  3.3 0.0 copy-start.1
  3.3 1.0 %copy-done.1 = bf16[2,3,3,64,64]{4,3,2,1,0:T(8,128)(2,1)S(1)} copy-done((bf16[2,3,3,64,64]{4,3,2,1,0:T(8,128)(2,1)S(1)}, bf16[2,3,3,64,64]{4,3,2,1,0:T(8,128)(2,1)}, u32[]{:S(2)}) %copy-start.1) | copy-done | bytes 147480
  4.3 32.6 %shard_map.64 = f32[2,8,256]{2,1,0:T(8,128)S(1)} custom-call(bf16[2,2,32,4096]{3,2,1,0:T(8,128)(2,1)S(1)} %copy-done, s32[12,2]{1,0:T(8,128)S(1)} %copy.7.pairs, f32[16,12]{1,0:T(8,128)S(1)} %copy-done.2, bf16[3,3,64,2]{3,2,1,0:T(8,128)(2,1)S(1)} %copy.8.w_first, bf16[2,3,3,64,64]{4,3,2,1,0:T(8,128)(2,1)S(1)} %copy-done.1, bf16[3,3,1,64]{3,2,1,0:T(2,128)(2,1)S(1)} %copy.9.w_last), custom_call_target="tpu_custom_call" | custom-call | tf_op jit(solution)/shard_map/pallas_call | solution.py:410
  36.9 0.6 %copy.11 = f32[2,8,256]{2,1,0:T(8,128)} copy(f32[2,8,256]{2,1,0:T(8,128)S(1)} %shard_map.64) | data formatting | bytes 32768
Async XLA Ops:
  0.0 0.7 %copy-start.4 = (s32[12,2]{0,1:T(2,128)S(1)}, s32[12,2]{0,1:T(2,128)}, u32[]{:S(2)}) copy-start(s32[12,2]{0,1:T(2,128)} %param.7) | copy-start | bytes 292
  0.7 0.7 %copy-start.3 = (bf16[3,3,64,2]{2,3,1,0:T(2,128)(2,1)S(1)}, bf16[3,3,64,2]{2,3,1,0:T(2,128)(2,1)}, u32[]{:S(2)}) copy-start(bf16[3,3,64,2]{2,3,1,0:T(2,128)(2,1)} %param.8) | copy-start | bytes 6916
  1.4 0.7 %copy-start.2 = (f32[16,12]{1,0:T(8,128)S(1)}, f32[16,12]{1,0:T(8,128)}, u32[]{:S(2)}) copy-start(f32[16,12]{1,0:T(8,128)} %inversion.1) | copy-start | bytes 2308
  2.1 1.2 %copy-start = (bf16[2,2,32,4096]{3,2,1,0:T(8,128)(2,1)S(1)}, bf16[2,2,32,4096]{3,2,1,0:T(8,128)(2,1)}, u32[]{:S(2)}) copy-start(bf16[2,2,32,4096]{3,2,1,0:T(8,128)(2,1)} %scenes.1) | copy-start | bytes 3145732
  3.3 1.0 %copy-start.1 = (bf16[2,3,3,64,64]{4,3,2,1,0:T(8,128)(2,1)S(1)}, bf16[2,3,3,64,64]{4,3,2,1,0:T(8,128)(2,1)}, u32[]{:S(2)}) copy-start(bf16[2,3,3,64,64]{4,3,2,1,0:T(8,128)(2,1)} %w_mid.1) | copy-start | bytes 442372

commit v2 on v1

--- a/solution.py
+++ b/solution.py
@@ -34,12 +34,17 @@
     n_date,
     n_strip,
     scenes,
+    pairs_hbm,
+    inversion_hbm,
+    w_first_hbm,
+    w_mid_hbm,
+    w_last_hbm,
+    out,
     pairs,
     inversion,
     w_first,
     w_mid,
     w_last,
-    out,
     tile,
     sendbuf,
     recvbuf,
@@ -93,8 +98,22 @@
     def _():
         pl.semaphore_signal(barrier, inc=1, device_id=(me, strip + 1), device_id_type=MESH)
 
-    load = pltpu.make_async_copy(scenes, tile, load_sem)
-    load.start()
+    loads = [
+        pltpu.make_async_copy(source, target, load_sem.at[i])
+        for i, (source, target) in enumerate(
+            (
+                (pairs_hbm, pairs),
+                (scenes, tile),
+                (w_first_hbm, w_first),
+                (w_mid_hbm, w_mid),
+                (w_last_hbm, w_last),
+                (inversion_hbm, inversion),
+            )
+        )
+    ]
+    for load in loads:
+        load.start()
+    loads[0].wait()
 
     upper, partner, own_date, sign = [], [], [], []
     for m in range(3):
@@ -105,8 +124,8 @@
 
         def pick(i, carry, m=m):
             date, is_ref = carry
-            ref = pairs[m * block + i, 0]
-            sec = pairs[m * block + i, 1]
+            ref = pairs[0, m * block + i]
+            sec = pairs[1, m * block + i]
             ref_hit = ref // date_dev == me
             sec_hit = sec // date_dev == me
             date = jnp.where(ref_hit, ref, jnp.where(sec_hit, sec, date))
@@ -118,7 +137,7 @@
         own_date.append(date - me * date_dev)
         sign.append(jnp.where(is_ref == 1, 1.0, -1.0).astype(F32))
 
-    load.wait()
+    loads[1].wait()
     pl.semaphore_wait(
         barrier,
         n_date - 1 + jnp.where(strip > 0, 1, 0) + jnp.where(strip < n_strip - 1, 1, 0),
@@ -148,18 +167,16 @@
 
     lax.fori_loop(0, span // 128, fill_select, 0)
 
+    for load in loads[2:]:
+        load.wait()
     base_first[...] = jnp.zeros_like(base_first)
-    nothing = jnp.zeros((64, 2), BF16)
-    eye_small = flag(iota((8, 2), 0) == iota((8, 2), 1)).astype(BF16)
     for b in range(4):
         for q in range(3):
-            stack = jnp.concatenate(
-                [w_first[b, q] if b < 3 else nothing, w_first[b - 1, q] if b > 0 else nothing],
-                axis=0,
-            )
-            turned = lax.dot_general(eye_small, stack, NT, preferred_element_type=F32)
             place = (b * 3 + q) * 2
-            base_first[place : place + 2, :] = turned[:2]
+            if b < 3:
+                base_first[place : place + 2, 0:64] = w_first[b, q].astype(F32)
+            if b > 0:
+                base_first[place : place + 2, 64:128] = w_first[b - 1, q].astype(F32)
     base = base_first[...].astype(BF16)
     k = iota((96, 32), 0)
     n = iota((96, 32), 1)
@@ -189,8 +206,7 @@
 
     rows_last[...] = jnp.zeros_like(rows_last)
     for p in range(3):
-        for q in range(3):
-            rows_last[p * 3 + q : p * 3 + q + 1, :] = w_last[p, q].astype(F32)
+        rows_last[p * 3 : p * 3 + 3, :] = w_last[p, 0].astype(F32)
     twice = flag((iota((64, 128), 1) & 63) == iota((64, 128), 0)).astype(BF16)
     both = jnp.dot(rows_last[...].astype(BF16), twice, preferred_element_type=F32).astype(BF16)
     k = iota((24, 16), 0)
@@ -382,8 +398,8 @@
 
         def add(i, acc, m=m):
             pair = m * block + i
-            ref = pairs[pair, 0] // date_dev
-            sec = pairs[pair, 1] // date_dev
+            ref = pairs[0, pair] // date_dev
+            sec = pairs[1, pair] // date_dev
             left = gathered[m, jnp.minimum(ref, sec)]
             right = gathered[m, jnp.maximum(ref, sec)]
             result = []
@@ -405,14 +421,26 @@
     cols = scenes.shape[3]
     span = cols // 2 + EDGE * LOOK_C
     vmem = pl.BlockSpec(memory_space=pltpu.VMEM)
-    smem = pl.BlockSpec(memory_space=pltpu.SMEM)
+    operands = (
+        scenes,
+        date_pairs.T,
+        inversion,
+        first_weight.transpose(0, 1, 3, 2),
+        mid_weight,
+        last_weight.transpose(0, 2, 1, 3),
+    )
     dma = pltpu.SemaphoreType.DMA
     return pl.pallas_call(
         functools.partial(kernel, n_date, n_strip),
         out_shape=jax.ShapeDtypeStruct((date_dev, 8, 256), F32),
-        in_specs=[pl.BlockSpec(memory_space=pl.ANY), smem, smem, vmem, vmem, vmem],
+        in_specs=[pl.BlockSpec(memory_space=pl.ANY)] * 6,
         out_specs=vmem,
         scratch_shapes=[
+            pltpu.SMEM(operands[1].shape, jnp.int32),
+            pltpu.SMEM(operands[2].shape, F32),
+            pltpu.VMEM(operands[3].shape, BF16),
+            pltpu.VMEM(operands[4].shape, BF16),
+            pltpu.VMEM(operands[5].shape, BF16),
             pltpu.VMEM(scenes.shape, BF16),
             pltpu.VMEM((3, 2, 2, 16, span), BF16),
             pltpu.VMEM((3, 2, 2, 16, span), BF16),
@@ -431,7 +459,7 @@
             pltpu.VMEM((WIN, 5 * 128), BF16),
             pltpu.VMEM((24, 256), F32),
             pltpu.VMEM((3, n_date, 8, 128), F32),
-            dma,
+            dma((6,)),
             dma((3, 2)),
             dma((3, 2)),
             dma((3, 2)),
@@ -440,9 +468,9 @@
             dma((3, n_date)),
         ],
         compiler_params=pltpu.CompilerParams(
-            collective_id=0, has_side_effects=True, vmem_limit_bytes=40 * 1024 * 1024
+            collective_id=0, has_side_effects=True, vmem_limit_bytes=60 * 1024 * 1024
         ),
-    )(scenes, date_pairs, inversion, first_weight, mid_weight, last_weight)
+    )(*operands)
 
 
 def solution(mesh):

time: 37.8 us -> 34.5 us (0.913)
  local copies, waits for them, and re-layouts: 4.88 us -> 1.32 us
    unnamed x14 -> x1, local copies, waits for them, and re-layouts: 4.88 us -> 1.32 us
where the time goes in v2:
time: 34.5 us; the launch traced here: 34.2 us
  Pallas kernels  32.9 us (95%)
  local copies, waits for them, and re-layouts  1.32 us (4%)
    pallas_call x1, Pallas kernels, per_device(): pl.pallas_call(functools.partial(kernel, n_date, n_strip), out_shape=jax....  32.9 us
    unnamed x1, local copies, waits for them, and re-layouts  1.32 us

profile of v2, /device:TPU:1, one launch (start us, length us, event | category | flops | bytes accessed | tf_op | source)
XLA Modules:
  0.0 34.2 jit_solution(39327189305340288)
XLA Ops:
  0.0 32.9 %shard_map.64 = f32[2,8,256]{2,1,0:T(8,128)} custom-call(bf16[2,2,32,4096]{3,2,1,0:T(8,128)(2,1)} %scenes.1, s32[2,12]{1,0:T(2,128)} %bitcast.5, f32[16,12]{1,0:T(8,128)} %inversion_hbm.1, bf16[3,3,2,64]{3,2,1,0:T(2,128)(2,1)} %bitcast.3, bf16[2,3,3,64,64]{4,3,2,1,0:T(8,128)(2,1)} %w_mid_hbm.1, bf16[3,1,3,64]{3,2,1,0:T(4,128)(2,1)} %bitcast.4), custom_call_target="tpu_custom_call" | custom-call | tf_op jit(solution)/shard_map/pallas_call | solution.py:433
  32.9 1.3 %copy.8 = f32[2,8,256]{2,1,0:T(8,128)} copy(f32[2,8,256]{2,1,0:T(8,128)} %shard_map.64) | data formatting | bytes 32768

commit v3 on v2

--- a/solution.py
+++ b/solution.py
@@ -45,7 +45,8 @@
     w_first,
     w_mid,
     w_last,
-    tile,
+    tile_0,
+    tile_1,
     sendbuf,
     recvbuf,
     select,
@@ -62,8 +63,12 @@
     hid_b,
     hid_c,
     last_out,
-    gathered,
+    gathered_0,
+    gathered_1,
+    gathered_2,
+    ready,
     load_sem,
+    tile_sem,
     ex_send,
     ex_recv,
     halo_send,
@@ -80,15 +85,28 @@
     bits = [0, 1, n_date.bit_length() - 2]
     total_rows = n_strip * 8
 
+    tile = (tile_0, tile_1)
+    gathered = (gathered_0, gathered_1, gathered_2)
+
     barrier = pltpu.get_barrier_semaphore()
 
-    def greet(j, carry):
-        pl.semaphore_signal(
-            barrier, inc=1, device_id=(lax.rem(me + j, n_date), strip), device_id_type=MESH
-        )
-        return carry
-
-    lax.fori_loop(1, n_date, greet, 0)
+    relayed = n_date == 8
+    if relayed:
+        greeted = 3
+        for bit in bits:
+            step = 1 << bit
+            other = me + step - 2 * step * lax.rem(me // step, 2)
+            pl.semaphore_signal(barrier, inc=1, device_id=(other, strip), device_id_type=MESH)
+    else:
+        greeted = n_date - 1
+
+        def greet(j, carry):
+            pl.semaphore_signal(
+                barrier, inc=1, device_id=(lax.rem(me + j, n_date), strip), device_id_type=MESH
+            )
+            return carry
+
+        lax.fori_loop(1, n_date, greet, 0)
 
     @pl.when(strip > 0)
     def _():
@@ -103,7 +121,6 @@
         for i, (source, target) in enumerate(
             (
                 (pairs_hbm, pairs),
-                (scenes, tile),
                 (w_first_hbm, w_first),
                 (w_mid_hbm, w_mid),
                 (w_last_hbm, w_last),
@@ -111,7 +128,17 @@
             )
         )
     ]
-    for load in loads:
+    tile_loads = [
+        pltpu.make_async_copy(
+            scenes.at[c, :, h * 16 : h * 16 + 16],
+            tile[h].at[c],
+            tile_sem.at[c, h],
+        )
+        for h in range(2)
+        for c in range(2)
+    ]
+    loads[0].start()
+    for load in tile_loads + loads[1:]:
         load.start()
     loads[0].wait()
 
@@ -137,18 +164,14 @@
         own_date.append(date - me * date_dev)
         sign.append(jnp.where(is_ref == 1, 1.0, -1.0).astype(F32))
 
-    loads[1].wait()
-    pl.semaphore_wait(
-        barrier,
-        n_date - 1 + jnp.where(strip > 0, 1, 0) + jnp.where(strip < n_strip - 1, 1, 0),
-    )
-
     exchange = {}
-    for m in (2, 0, 1):
-        offset = pl.multiple_of((1 - upper[m]) * (cols - span), 128)
-        for h in range(2):
+    for h in range(2):
+        for load in tile_loads[2 * h : 2 * h + 2]:
+            load.wait()
+        for m in range(3):
+            offset = pl.multiple_of((1 - upper[m]) * (cols - span), 128)
             for c in range(2):
-                sendbuf[m, h, c] = tile[c, own_date[m], h * 16 : h * 16 + 16, pl.ds(offset, span)]
+                sendbuf[m, h, c] = tile[h][c, own_date[m], :, pl.ds(offset, span)]
             exchange[m, h] = pltpu.make_async_remote_copy(
                 src_ref=sendbuf.at[m, h],
                 dst_ref=recvbuf.at[m, h],
@@ -157,7 +180,13 @@
                 device_id=(partner[m], strip),
                 device_id_type=MESH,
             )
-            exchange[m, h].start()
+        if h == 0:
+            pl.semaphore_wait(
+                barrier,
+                greeted + jnp.where(strip > 0, 1, 0) + jnp.where(strip < n_strip - 1, 1, 0),
+            )
+            for m in (2, 0, 1):
+                exchange[m, h].start()
 
     def fill_select(j, carry):
         apart = iota((128, 256), 0) + j * 128 - LOOK_C * iota((128, 256), 1)
@@ -167,7 +196,7 @@
 
     lax.fori_loop(0, span // 128, fill_select, 0)
 
-    for load in loads[2:]:
+    for load in loads[1:]:
         load.wait()
     base_first[...] = jnp.zeros_like(base_first)
     for b in range(4):
@@ -255,11 +284,10 @@
         own_offset = pl.multiple_of(upper[m] * (cols - span), 128)
 
         def columns(start, width):
-            rows = slice(h * 16, h * 16 + 16)
             own = pl.ds(pl.multiple_of(own_offset + start, 128), width)
             there = pl.ds(start, width)
-            a0 = tile[0, own_date[m], rows, own].astype(F32)
-            a1 = tile[1, own_date[m], rows, own].astype(F32)
+            a0 = tile[h][0, own_date[m], :, own].astype(F32)
+            a1 = tile[h][1, own_date[m], :, own].astype(F32)
             b0 = recvbuf[m, h, 0, :, there].astype(F32)
             b1 = recvbuf[m, h, 1, :, there].astype(F32)
             fields = (
@@ -316,8 +344,8 @@
 
     def peer_copy(m, j):
         return pltpu.make_async_remote_copy(
-            src_ref=gathered.at[m, me],
-            dst_ref=gathered.at[m, me],
+            src_ref=gathered[m].at[me],
+            dst_ref=gathered[m].at[me],
             send_sem=ga_send.at[m, j],
             recv_sem=ga_recv.at[m, j],
             device_id=(lax.rem(me + j, n_date), strip),
@@ -335,8 +363,8 @@
 
         x = xs[m]
         x = jnp.concatenate([pltpu.roll(x, 1, 1), x, pltpu.roll(x, 255, 1)], axis=0)
-        x = x.astype(BF16)
-        wide = lax.dot_general(x, big_first[...], TN, preferred_element_type=F32)[:WIN]
+        x = x[:, :WIN].astype(BF16)
+        wide = lax.dot_general(x, big_first[...], TN, preferred_element_type=F32)
         for i in range(7):
             spread(hid_a, i, masked(m, wide[:, i * 128 : i * 128 + 128], i, -3))
         for layer, (source, count) in enumerate(((hid_a, 6), (hid_b, 5))):
@@ -357,7 +385,7 @@
             + pltpu.roll(last_out[8:16], 256 - EDGE, 1)
             + pltpu.roll(last_out[16:24], 256 - (EDGE + 1), 1)
         )[:, :128]
-        gathered[m, me] = phase.astype(BF16).astype(F32)
+        gathered[m][me] = phase.astype(BF16).astype(F32)
 
         def tell(j, carry):
             peer_copy(m, j).start()
@@ -365,43 +393,39 @@
 
         lax.fori_loop(1, n_date, tell, 0)
 
-    for m in (0, 1):
-        for h in range(2):
-            exchange[m, h].wait_recv()
-            look(m, h)
+    exchange[0, 0].wait_send()
+    for m in (2, 0, 1):
+        exchange[m, 1].start()
+    for h, m in ((0, 0), (0, 1), (1, 0), (1, 1)):
+        exchange[m, h].wait_recv()
+        if relayed and (m, h) == (1, 0):
+            pl.semaphore_signal(ready, inc=1, device_id=(partner[0], strip), device_id_type=MESH)
+        look(m, h)
+    if relayed:
+        pl.semaphore_wait(ready, 1)
     network(0)
-    network(1)
     for h in range(2):
         exchange[2, h].wait_recv()
         look(2, h)
+    network(1)
     network(2)
-
-    for m in range(3):
-        for h in range(2):
-            exchange[m, h].wait_send()
-
-            @pl.when(strip > 0 if h == 0 else strip < n_strip - 1)
-            def _(m=m, h=h):
-                halo(m, h).wait_send()
-
-        def hear(j, carry, m=m):
-            copy = peer_copy(m, j)
-            copy.wait_send()
-            copy.wait_recv()
-            return carry
-
-        lax.fori_loop(1, n_date, hear, 0)
 
     zero = jnp.zeros((8, 128), F32)
     acc = (zero,) * (2 * date_dev)
     for m in range(3):
+
+        def hear(j, carry, m=m):
+            peer_copy(m, j).wait_recv()
+            return carry
+
+        lax.fori_loop(1, n_date, hear, 0)
 
         def add(i, acc, m=m):
             pair = m * block + i
             ref = pairs[0, pair] // date_dev
             sec = pairs[1, pair] // date_dev
-            left = gathered[m, jnp.minimum(ref, sec)]
-            right = gathered[m, jnp.maximum(ref, sec)]
+            left = gathered[m][jnp.minimum(ref, sec)]
+            right = gathered[m][jnp.maximum(ref, sec)]
             result = []
             for t in range(date_dev):
                 gain = inversion[me * date_dev + t, pair]
@@ -412,6 +436,21 @@
     for t in range(date_dev):
         out[t, :, 0:128] = acc[2 * t]
         out[t, :, 128:256] = acc[2 * t + 1]
+
+    for m in range(3):
+        for h in range(2):
+            if (m, h) != (0, 0):
+                exchange[m, h].wait_send()
+
+            @pl.when(strip > 0 if h == 0 else strip < n_strip - 1)
+            def _(m=m, h=h):
+                halo(m, h).wait_send()
+
+        def sent(j, carry, m=m):
+            peer_copy(m, j).wait_send()
+            return carry
+
+        lax.fori_loop(1, n_date, sent, 0)
 
 
 def per_device(scenes, date_pairs, first_weight, mid_weight, last_weight, inversion):
@@ -441,7 +480,7 @@
             pltpu.VMEM(operands[3].shape, BF16),
             pltpu.VMEM(operands[4].shape, BF16),
             pltpu.VMEM(operands[5].shape, BF16),
-            pltpu.VMEM(scenes.shape, BF16),
+            *(pltpu.VMEM((2, date_dev, 16, cols), BF16),) * 2,
             pltpu.VMEM((3, 2, 2, 16, span), BF16),
             pltpu.VMEM((3, 2, 2, 16, span), BF16),
             pltpu.VMEM((span, 256), BF16),
@@ -458,8 +497,10 @@
             pltpu.VMEM((6 * WIN, 384), BF16),
             pltpu.VMEM((WIN, 5 * 128), BF16),
             pltpu.VMEM((24, 256), F32),
-            pltpu.VMEM((3, n_date, 8, 128), F32),
-            dma((6,)),
+            *(pltpu.VMEM((n_date, 8, 128), F32),) * 3,
+            pltpu.SemaphoreType.REGULAR,
+            dma((5,)),
+            dma((2, 2)),
             dma((3, 2)),
             dma((3, 2)),
             dma((3, 2)),

time: 34.5 us -> 33.7 us (0.977)
  the two profiles are of different devices: /device:TPU:1 before, /device:TPU:0 now
where the time goes in v3:
time: 33.7 us; the launch traced here: 33.5 us
  Pallas kernels  32.2 us (96%)
  local copies, waits for them, and re-layouts  1.32 us (4%)
    pallas_call x1, Pallas kernels, per_device(): pl.pallas_call(functools.partial(kernel, n_date, n_strip), out_shape=jax....  32.2 us
    unnamed x1, local copies, waits for them, and re-layouts  1.32 us

profile of v3, /device:TPU:0, one launch (start us, length us, event | category | flops | bytes accessed | tf_op | source)
XLA Modules:
  0.0 33.5 jit_solution(7220718368475363408)
XLA Ops:
  0.0 32.2 %shard_map.64 = f32[2,8,256]{2,1,0:T(8,128)} custom-call(bf16[2,2,32,4096]{3,2,1,0:T(8,128)(2,1)} %scenes.1, s32[2,12]{1,0:T(2,128)} %bitcast.5, f32[16,12]{1,0:T(8,128)} %inversion_hbm.1, bf16[3,3,2,64]{3,2,1,0:T(2,128)(2,1)} %bitcast.3, bf16[2,3,3,64,64]{4,3,2,1,0:T(8,128)(2,1)} %w_mid_hbm.1, bf16[3,1,3,64]{3,2,1,0:T(4,128)(2,1)} %bitcast.4), custom_call_target="tpu_custom_call" | custom-call | tf_op jit(solution)/shard_map/pallas_call | solution.py:472
  32.2 1.3 %copy.8 = f32[2,8,256]{2,1,0:T(8,128)} copy(f32[2,8,256]{2,1,0:T(8,128)} %shard_map.64) | data formatting | bytes 32768
